TPU v7x, 32 devices: a whole 2x2x4 slice. The times are simulated.
32 devices in a mesh: rep: 2 (over x), fsdp: 4 (over z), ctx: 4 (over y, core).
Axes of the slice: x: 2, y: 2, z: 4, core: 2. Of those that a mesh axis runs over, the one named last changes fastest.
Arguments:
- tokens: bfloat16 [8, 1024, 768], P(('rep', 'fsdp'), 'ctx'), may hold values from -2.5 to 2.5
- lengths: int32 [8], P(('rep', 'fsdp')), may hold values from 256 to 1024, as said below
- cotangent: bfloat16 [8, 1024, 768], P(('rep', 'fsdp'), 'ctx'), may hold values from -8 to 8
- w_qkv: bfloat16 [2, 3, 768, 768], P(None, None, 'fsdp'), may hold values from -0.21875 to 0.21875
- w_attn_out: bfloat16 [2, 768, 768], P(None, 'fsdp'), may hold values from -1.1953125 to 1.1953125
- w_in: bfloat16 [2, 768, 3072], P(None, 'fsdp'), may hold values from -0.21875 to 0.21875
- w_out: bfloat16 [2, 3072, 768], P(None, 'fsdp'), may hold values from -0.109375 to 0.109375
- bias_q: bfloat16 [2, 768], P(None, 'fsdp'), may hold values from -0.75 to 0.75
- bias_d: bfloat16 [2, 3, 768], P(None, None, 'fsdp'), may hold values from -0.25 to 0.25
- bias_ff: bfloat16 [2, 3072], P(None, 'fsdp'), may hold values from -0.75 to 0.75
- norm_gain: bfloat16 [2, 2, 768], P(None, None, 'fsdp'), may hold values from 0.5 to 1.5
- norm_shift: bfloat16 [2, 2, 768], P(None, None, 'fsdp'), may hold values from -0.75 to 0.75
Outputs:
- output_tokens: bfloat16 [8, 1024, 768], P(('rep', 'fsdp'), 'ctx')
- grad_tokens: float32 [8, 1024, 768], P(('rep', 'fsdp'), 'ctx')
- grad_w_qkv: float32 [2, 3, 768, 768], P(None, None, 'fsdp')
- grad_w_attn_out: float32 [2, 768, 768], P(None, 'fsdp')
- grad_w_in: float32 [2, 768, 3072], P(None, 'fsdp')
- grad_w_out: float32 [2, 3072, 768], P(None, 'fsdp')
- grad_bias_q: float32 [2, 768], P(None, 'fsdp')
- grad_bias_d: float32 [2, 3, 768], P(None, None, 'fsdp')
- grad_bias_ff: float32 [2, 3072], P(None, 'fsdp')
- grad_norm_gain: float32 [2, 2, 768], P(None, None, 'fsdp')
- grad_norm_shift: float32 [2, 2, 768], P(None, None, 'fsdp')
Inputs may be any that keep to these rules, and one draw needn't show every extreme that they name: `lengths`: some sequence has exactly 1024 valid tokens and some other exactly 256.
All inputs are finite; a program needn't handle non-finite values.
Results may differ from a plain program's by a relative error of at most 0.02.
Values may be sent and summed in bfloat16 or wider, within the bound.
A program may use at most 256 MiB of HBM per device.

v0:
```python
import functools

import jax
import jax.numpy as jnp
from jax import lax
from jax.experimental import pallas as pl
from jax.experimental.pallas import tpu as pltpu
from jax.sharding import PartitionSpec as P

HEADS = 12
HEAD = 64
D = HEADS * HEAD
MESH = pl.DeviceIdType.MESH
BF = jnp.bfloat16
F32 = jnp.float32
MIB = 2**20
GATHER_CUT, REDUCE_CUT = 1, 3

epsilon = 1e-05
score_scale = 0.125
masked_value = -1e30


class Place:
    def __init__(self, n, ny):
        self.n, self.ny = n, ny
        self.r = lax.axis_index("rep")
        self.z = lax.axis_index("fsdp")
        self.c = lax.axis_index("ctx")
        self.y, self.k = lax.div(self.c, 2), lax.rem(self.c, 2)
        self.e = lax.rem(self.y, 2)
        self.q = 2 * self.e + self.r
        self.qx = 2 * self.e + (1 - self.r)
        self.qy = 2 * (1 - self.e) + self.r
        self.qd = 2 * (1 - self.e) + (1 - self.r)

    def shard(self, offset):
        return lax.rem(self.z + (offset + self.n), self.n)

    def up(self, offset):
        return (self.r, self.shard(offset), self.c)

    def x(self):
        return (1 - self.r, self.z, self.c)

    def across(self):
        return (self.r, self.z, 2 * (self.y + 1 - 2 * self.e) + self.k)

    def row(self, offset, flip=0):
        y = lax.rem(self.y + offset, self.ny)
        k = self.k + flip * (1 - 2 * self.k)
        return (self.r, self.z, 2 * y + k)

    def core(self):
        return self.row(0, 1)

    def greet(self):
        others = [self.up(o) for o in range(1, self.n)]
        others += [self.x(), self.core()]
        others += [self.row(o) for o in range(1, self.ny)]
        barrier = pltpu.get_barrier_semaphore()
        for other in others:
            pl.semaphore_signal(barrier, inc=1, device_id=other, device_id_type=MESH)
        pl.semaphore_wait(barrier, len(others))


def remote(src, dst, send, recv, device):
    copy = pltpu.make_async_remote_copy(
        src_ref=src, dst_ref=dst, send_sem=send, recv_sem=recv, device_id=device, device_id_type=MESH
    )
    copy.start()
    return copy


def cut(half, sixths):
    first = max(8, half * sixths // 96 * 16)
    return [(0, first), (first, half - first)]


class Gather:
    def __init__(self, place, full, by_shard, local, send, recv):
        self.place, self.full, self.by_shard = place, full, by_shard
        self.local, self.send, self.recv = local, send, recv
        self.n = place.n
        self.half = full.shape[2] // 2
        self.pieces = cut(self.half, GATHER_CUT)
        self.copies, self.core_copies = [], []

    @staticmethod
    def count(n):
        return 10 * (n - 1)

    def part(self, shard, q, piece=None):
        start, size = (0, self.half) if piece is None else piece
        rows = pl.ds(pl.multiple_of(self.place.k * self.half + start, 8), size)
        return self.full.at[shard, q, rows] if self.by_shard else self.full.at[q, shard, rows]

    def load(self, sources):
        self.loads = []
        z = self.place.z
        for i, (q, count, source) in enumerate(sources):
            if self.by_shard:
                target = self.full.at[z]
            elif count is None:
                target = self.full.at[q, z]
            else:
                target = self.full.at[pl.ds(q, count), z]
            copy = pltpu.make_async_copy(source, target, self.local.at[i])
            copy.start()
            self.loads.append(copy)

    def share(self, kind, offset, piece, device):
        slot = kind * (self.n - 1) + offset - 1
        copy = remote(piece, piece, self.send.at[slot], self.recv.at[slot], device)
        self.copies.append(copy)
        return copy

    def core_share(self, kind, offset, piece):
        copy = self.share(5 + kind, offset, piece, self.place.core())
        self.core_copies.append(copy)

    def start(self):
        place = self.place
        for copy in self.loads:
            copy.wait()
        mine = self.part(place.z, place.q)
        self.ups = [self.share(0, o, mine, place.up(o)) for o in range(1, self.n)]

    def to_x(self):
        place = self.place
        self.xs = []
        for o in range(1, self.n):
            self.ups[o - 1].wait_recv()
            piece = self.part(place.shard(-o), place.q)
            self.xs.append(self.share(1, o, piece, place.x()))
            self.core_share(0, o, piece)

    def to_y(self):
        place = self.place
        self.ys = [
            self.share(2, o, self.part(place.shard(-o), place.q), place.across()) for o in range(1, self.n)
        ]

    def from_x(self):
        place = self.place
        self.dys = []
        for o in range(1, self.n):
            shard = place.shard(-o)
            self.xs[o - 1].wait_recv()
            self.dys.append(self.share(3, o, self.part(shard, place.qx, self.pieces[0]), place.across()))
            self.core_share(1, o, self.part(shard, place.qx))

    def from_y(self):
        place = self.place
        self.dxs = []
        for o in range(1, self.n):
            shard = place.shard(-o)
            self.ys[o - 1].wait_recv()
            self.dxs.append(self.share(4, o, self.part(shard, place.qy, self.pieces[1]), place.x()))
            self.core_share(2, o, self.part(shard, place.qy))

    def last(self):
        place = self.place
        for o in range(1, self.n):
            shard = place.shard(-o)
            self.dys[o - 1].wait_recv()
            self.core_share(3, o, self.part(shard, place.qd, self.pieces[0]))
        for o in range(1, self.n):
            shard = place.shard(-o)
            self.dxs[o - 1].wait_recv()
            self.core_share(4, o, self.part(shard, place.qd, self.pieces[1]))

    def finish(self):
        for copy in self.core_copies:
            copy.wait_recv()

    def drain(self):
        for copy in self.copies:
            copy.wait_send()

    def steps(self):
        return dict(A=self.start, B=self.to_x, Y=self.to_y, C=self.from_x, E=self.from_y, L=self.last, F=self.finish)


def weight_sources(b, qkv, ao, win, wout):
    return [
        [(0, 3, qkv.at[b]), (3, None, ao.at[b])],
        [(q, None, win.at[b, :, pl.ds(q * D, D)]) for q in range(4)],
        [(None, None, wout.at[b])],
    ]


class Reduce:
    def __init__(self, place, grad, landing, out, wide, local, send, recv, credit):
        self.place, self.grad, self.out, self.wide = place, grad, out, wide
        self.core_in, self.x_in, self.y_in, self.dx_in, self.dy_in, self.z_in, self.far_in = landing
        self.local, self.send, self.recv, self.credit = local, send, recv, credit
        self.n, self.ny = place.n, place.ny
        self.half = grad.shape[2] // 2
        self.low, self.top = cut(self.half, REDUCE_CUT)
        self.copies, self.cored, self.owns = [], [], []
        self.slot = 0
        self.plan = [self.add_cores, self.plane, self.depth, self.total, self.turn, self.last]

    @staticmethod
    def count(n, ny):
        return 4 + 6 + (n - 1) + (ny // 2 - 1) + 9

    @staticmethod
    def landing_buffers(n, ny):
        half = D // n // 2
        (_, second), (_, first) = cut(half, REDUCE_CUT)
        return [
            pltpu.VMEM((n, 4, half, D), BF),
            pltpu.VMEM((n, half, D), BF),
            pltpu.VMEM((n, half, D), BF),
            pltpu.VMEM((n, first, D), BF),
            pltpu.VMEM((n, second, D), BF),
            pltpu.VMEM((n - 1, half, D), BF),
            pltpu.VMEM((max(1, ny // 2 - 1), half, D), BF),
        ]

    def peers(self):
        place = self.place
        others = [place.up(o) for o in range(1, self.n)] + [place.x(), place.across(), place.core()]
        return others + [place.row(2 * i + 2) for i in range(self.ny // 2 - 1)]

    def release(self):
        for other in self.peers():
            pl.semaphore_signal(self.credit, inc=1, device_id=other, device_id_type=MESH)

    def acquire(self):
        pl.semaphore_wait(self.credit, len(self.peers()))

    def share(self, src, dst, device):
        copy = remote(src, dst, self.send.at[self.slot], self.recv.at[self.slot], device)
        self.slot += 1
        self.copies.append(copy)
        return copy

    def rows(self, k, piece=None):
        start, size = (0, self.half) if piece is None else piece
        return pl.ds(pl.multiple_of(k * self.half + start, 8), size)

    def own(self, shards, q, piece=None):
        return self.grad.at[shards, q, self.rows(self.place.k, piece)]

    def core(self, shards, q):
        source = self.grad.at[shards, q, self.rows(1 - self.place.k)]
        self.cored.append(self.share(source, self.core_in.at[shards, q], self.place.core()))

    def add_into(self, target, *sources):
        total = target[...].astype(F32)
        for source in sources:
            total = total + source[...].astype(F32)
        target[...] = total.astype(BF)

    def add_cores(self):
        for copy in self.cored:
            copy.wait_recv()

        def one(i, _):
            shard, q = lax.div(i, 4), lax.rem(i, 4)
            self.add_into(self.own(shard, q), self.core_in.at[shard, q])
            return 0

        lax.fori_loop(0, 4 * self.n, one, 0)
        place, every = self.place, slice(None)
        top, low = pl.ds(*self.top), pl.ds(*self.low)
        self.dx = self.share(self.own(every, place.qd, self.top), self.dx_in, place.x())
        self.dy = self.share(self.own(every, place.qd, self.low), self.dy_in, place.across())
        self.planes = [
            self.share(self.own(every, place.qx, self.top), self.x_in.at[:, top], place.x()),
            self.share(self.own(every, place.qy, self.low), self.y_in.at[:, low], place.across()),
        ]

    def plane(self):
        place, every = self.place, slice(None)
        top, low = pl.ds(*self.top), pl.ds(*self.low)
        self.dx.wait_recv()

        def one(j, _):
            self.add_into(self.own(j, place.qy, self.top), self.dx_in.at[j])
            return 0

        lax.fori_loop(0, self.n, one, 0)
        self.planes.append(
            self.share(self.own(every, place.qy, self.top), self.y_in.at[:, top], place.across())
        )
        self.dy.wait_recv()

        def two(j, _):
            self.add_into(self.own(j, place.qx, self.low), self.dy_in.at[j])
            return 0

        lax.fori_loop(0, self.n, two, 0)
        self.planes.append(self.share(self.own(every, place.qx, self.low), self.x_in.at[:, low], place.x()))

    def depth(self):
        place = self.place
        for copy in self.planes:
            copy.wait_recv()

        def one(j, _):
            self.add_into(self.own(j, place.q), self.x_in.at[j], self.y_in.at[j])
            return 0

        lax.fori_loop(0, self.n, one, 0)
        self.deep = [
            self.share(self.own(place.shard(o), place.q), self.z_in.at[o - 1], place.up(o))
            for o in range(1, self.n)
        ]

    def mine(self, q, piece=None):
        rows = self.rows(self.place.k, piece)
        if self.wide:
            return self.out.at[rows, pl.ds(pl.multiple_of(q * D, D), D)]
        return self.out.at[q, rows]

    def total(self):
        place = self.place
        for copy in self.deep:
            copy.wait_recv()
        own = self.own(place.z, place.q)
        self.add_into(own, *[self.z_in.at[o - 1] for o in range(1, self.n)])
        if self.ny > 2:
            far = [self.share(own, self.far_in.at[i], place.row(2 * i + 2)) for i in range(self.ny // 2 - 1)]
            for copy in far:
                copy.wait_recv()
            mine = own[...].astype(F32)
            terms = [mine] + [self.far_in[i].astype(F32) for i in range(self.ny // 2 - 1)]
            total = jnp.zeros_like(mine)
            for y in range(0, self.ny, 2):
                offset = lax.rem(place.y - place.e - y + self.ny, self.ny)
                for i, term in enumerate(terms):
                    total = total + jnp.where(offset == 2 * i, term, 0.0)
            for copy in far:
                copy.wait_send()
            self.copies = [copy for copy in self.copies if all(copy is not other for other in far)]
            own[...] = total.astype(BF)
        copy = pltpu.make_async_copy(own, self.mine(place.q), self.local)
        copy.start()
        self.owns.append(copy)
        self.spread = [
            self.share(own, self.mine(place.q), place.x()),
            self.share(own, self.mine(place.q), place.across()),
        ]
        self.cores = [self.share(own, self.mine(place.q), place.core())]

    def forward(self, q, device, piece=None):
        return self.share(self.mine(q, piece), self.mine(q, piece), device)

    def turn(self):
        place = self.place
        self.spread[0].wait_recv()
        self.dy = self.forward(place.qx, place.across(), self.top)
        self.cores.append(self.forward(place.qx, place.core()))
        self.spread[1].wait_recv()
        self.dx = self.forward(place.qy, place.x(), self.low)
        self.cores.append(self.forward(place.qy, place.core()))

    def last(self):
        place = self.place
        self.dy.wait_recv()
        self.cores.append(self.forward(place.qd, place.core(), self.top))
        self.dx.wait_recv()
        self.cores.append(self.forward(place.qd, place.core(), self.low))

    def finish(self):
        for copy in self.cores:
            copy.wait_recv()

    def drain(self):
        for copy in self.copies:
            copy.wait_send()
        for copy in self.owns:
            copy.wait()
        self.copies, self.owns = [], []


class SmallReduce:
    def __init__(self, place, total, landing, send, recv):
        self.place, self.total, self.landing, self.send, self.recv = place, total, landing, send, recv
        n, ny = place.n, place.ny
        self.stages = [
            [place.core()],
            [place.up(o) for o in range(1, n)],
            [place.x()],
            [place.row(o) for o in range(1, ny)],
        ]
        self.copies = []
        self.slot = 0

    @staticmethod
    def count(n, ny):
        return 1 + (n - 1) + 1 + (ny - 1)

    def start(self, stage):
        self.current = []
        for device in self.stages[stage]:
            slot = self.slot
            copy = remote(
                self.total.at[stage], self.landing.at[slot], self.send.at[slot], self.recv.at[slot], device
            )
            self.current.append((slot, copy))
            self.copies.append(copy)
            self.slot += 1

    def end(self, stage):
        place, ny = self.place, self.place.ny
        for _, copy in self.current:
            copy.wait_recv()
        terms = [self.total[stage]] + [self.landing[slot] for slot, _ in self.current]
        if stage == 3 and ny > 2:
            total = jnp.zeros_like(terms[0])
            for y in range(ny):
                offset = lax.rem(place.y - y + ny, ny)
                for o in range(ny):
                    total = total + jnp.where(offset == o, terms[o], 0.0)
        else:
            total = functools.reduce(lambda a, b: a + b, terms)
        self.total[stage + 1] = total

    def steps(self):
        out = [functools.partial(self.start, 0)]
        for stage in range(4):
            out.append(functools.partial(self.end, stage))
            if stage < 3:
                out.append(functools.partial(self.start, stage + 1))
        return out


def matmul(operand_a, operand_b):
    return jnp.dot(operand_a, operand_b, preferred_element_type=F32)


def matmul_left_t(operand_a, operand_b):
    return lax.dot_general(operand_a, operand_b, (((0,), (0,)), ((), ())), preferred_element_type=F32)


def matmul_right_t(operand_a, operand_b):
    return lax.dot_general(operand_a, operand_b, (((1,), (1,)), ((), ())), preferred_element_type=F32)


def unit(ref, index, columns=None):
    block = ref[index] if columns is None else ref[index, :, :, columns]
    return block.reshape(D, block.shape[-1])


def center_scale(rows):
    center = rows - jnp.mean(rows, axis=-1, keepdims=True)
    inverse = lax.rsqrt(jnp.mean(center * center, axis=-1, keepdims=True) + epsilon)
    return center * inverse, inverse


class Exchange:
    def __init__(self, place, kv, send, recv):
        self.place, self.kv, self.send, self.recv = place, kv, send, recv
        self.copies = []

    @staticmethod
    def count(ny):
        return 2 * ny

    def share(self, half, chip_row, slot, device):
        part = self.kv.at[:, half, 2 * chip_row + self.place.k]
        copy = remote(part, part, self.send.at[half, slot], self.recv.at[half, slot], device)
        self.copies.append(copy)
        return copy

    def start(self, half):
        place, ny = self.place, self.place.ny
        far = [self.share(half, place.y, o, place.row(o)) for o in range(1, ny)]
        near = [self.share(half, place.y, 0, place.core())]
        return far, near

    def forward(self, half, state):
        place, ny = self.place, self.place.ny
        far, near = state
        for o in range(1, ny):
            far[o - 1].wait_recv()
            near.append(self.share(half, lax.rem(place.y - o + ny, ny), ny + o - 1, place.core()))

    def finish(self, state):
        for copy in state[1]:
            copy.wait_recv()

    def drain(self):
        for copy in self.copies:
            copy.wait_send()


def spread_small(n, small_full, wide_full, narrow, wide):
    width = small_full.shape[2]
    row = lax.broadcasted_iota(jnp.int32, (width, D), 0)
    column = lax.broadcasted_iota(jnp.int32, (width, D), 1)
    total = 0.0
    for j in range(n):
        place = jnp.where(column - row == j * width, 1.0, 0.0).astype(BF)
        total = total + matmul(small_full[j], place)
    narrow[...] = total
    turns = n // 4
    for c in range(4):
        if turns == 1:
            total = wide_full[c].astype(F32)
        else:
            row = lax.broadcasted_iota(jnp.int32, (4 * width, D), 0)
            column = lax.broadcasted_iota(jnp.int32, (4 * width, D), 1)
            total = 0.0
            for t in range(turns):
                place = jnp.where(column - row == t * 4 * width, 1.0, 0.0).astype(BF)
                total = total + matmul(wide_full[c * turns + t], place)
        for b in range(2):
            wide[b, c : c + 1] = total[b : b + 1]


def side_mask(side):
    lane = lax.broadcasted_iota(jnp.int32, (1, 2 * HEAD), 1)
    inside = lane < HEAD if side == 0 else lane >= HEAD
    return jnp.where(inside, 1.0, 0.0).astype(BF)


def attend(query, kv, half, mask, out, stats, first_head):
    rows = query.shape[0]
    lane = lax.broadcasted_iota(jnp.int32, (rows, 2 * HEAD), 1)
    allowed = mask[0:1]

    def pair(p, _):
        columns = pl.ds(pl.multiple_of(p * 2 * HEAD, 2 * HEAD), 2 * HEAD)
        where = pl.ds(pl.multiple_of(half * (D // 2) + p * 2 * HEAD, 2 * HEAD), 2 * HEAD)
        keys = kv[0, half, :, :, columns].reshape(-1, 2 * HEAD)
        values = kv[1, half, :, :, columns].reshape(-1, 2 * HEAD)
        query_pair = query[:, where]
        mixed = []
        for side in range(2):
            scores = matmul_right_t(query_pair * side_mask(side), keys) + allowed
            peak = jnp.max(scores, axis=-1, keepdims=True)
            weight = jnp.exp(scores - peak)
            total = jnp.sum(weight, axis=-1, keepdims=True)
            mixed.append(matmul((weight / total).astype(BF), values))
            head = first_head + 2 * p + side
            stats[...] = jnp.where(lane == head, peak + jnp.log(total), stats[...])
        out[:, where] = jnp.where(lane < HEAD, mixed[0], mixed[1])
        return 0

    lax.fori_loop(0, HEADS // 4, pair, 0)


SCHEDULE = [
    "A0 B0 Y0 A1",
    [
        "C0 E0 B1 Y1 A2 L0 C1 E1 B2 Y2 A3 F0",
        "L1 C2 E2 B3 Y3 A4",
        "F1 L2",
        "C3 E3 B4 Y4",
        "A5 F2",
        "L3",
        "C4 E4",
        "B5 Y5",
        "F3",
        "",
    ],
    ["L4", "C5 E5 F4", "L5", "F5", "", "", "", "", "", ""],
]

SAVED = ("x", "query", "mixed", "stats", "hat_one", "active", "slope", "hat_two")


def forward_kernel(n, ny, *refs):
    tokens, mask, qkv, ao, win, wout, query_bias, bias_rows, wide_bias, gains, shifts = refs[:11]
    refs = refs[11:]
    outs = refs[:6]
    kv_outs, saved_outs = refs[6:8], refs[8:16]
    narrow_out, wide_out, result = refs[16:19]
    refs = refs[19:]
    fulls, kvs, saved = refs[:6], refs[6:8], refs[8:16]
    carried, normed, normed_bf, small_full, wide_full, small_rows, wide_rows = refs[16:23]
    local, send, recv, small_send, small_recv, kv_send, kv_recv, save_sem = refs[23:]
    place = Place(n, ny)
    groups = []
    for g in range(6):
        b, kind = g // 3, g % 3
        group = Gather(place, fulls[g], kind == 2, local.at[g], send.at[g], recv.at[g])
        group.load(weight_sources(b, qkv, ao, win, wout)[kind])
        groups.append(group)
    small_rows[0:2] = query_bias[...].astype(F32)
    for b in range(2):
        small_rows[2 + 3 * b : 5 + 3 * b] = bias_rows[b].astype(F32)
        small_rows[8 + 2 * b : 10 + 2 * b] = gains[b].astype(F32)
        small_rows[12 + 2 * b : 14 + 2 * b] = shifts[b].astype(F32)
    wide_rows[...] = jnp.zeros_like(wide_rows)
    wide_rows[0:2] = wide_bias[...].astype(F32)
    small_full[place.z] = small_rows[...].astype(BF)
    wide_full[place.z] = wide_rows[...].astype(BF)
    place.greet()
    smalls = []
    for i, ref in enumerate((small_full, wide_full)):
        own = ref.at[place.z]
        smalls += [
            remote(own, own, small_send.at[i, o], small_recv.at[i, o], place.up(o)) for o in range(1, n)
        ]
    kept = []

    def keep(source, target, sem):
        copy = pltpu.make_async_copy(source, target, sem)
        copy.start()
        kept.append(copy)

    plans = [group.steps() for group in groups]

    def run(steps):
        for name in steps.split():
            g = int(name[1])
            plans[g].pop(name[0])()
            if name[0] == "F":
                keep(fulls[g], outs[g], local.at[g, 4])

    carried[...] = tokens[...].astype(F32)
    run(SCHEDULE[0])
    for copy in smalls:
        copy.wait_recv()
    spread_small(n, small_full, wide_full, narrow_out, wide_out)
    x, query, mixed, stats, hat_one, active, slope, hat_two = saved
    for b in range(2):
        first, second, third = fulls[3 * b : 3 * b + 3]

        def save(*names):
            for name in names:
                i = SAVED.index(name)
                keep(saved[i].at[b], saved_outs[i].at[b], save_sem.at[b, i])

        turn = iter(SCHEDULE[1 + b])
        run(next(turn))
        x[b] = carried[...].astype(BF)
        exchange = Exchange(place, kvs[b], kv_send.at[b], kv_recv.at[b])
        states = []
        for half in range(2):
            columns = slice(half * (D // 2), (half + 1) * (D // 2))
            kvs[b][0, half, place.c] = matmul(x[b], unit(first, 1, columns)).astype(BF)
            value_bias = narrow_out[2 + 3 * b : 3 + 3 * b, columns]
            kvs[b][1, half, place.c] = (matmul(x[b], unit(first, 2, columns)) + value_bias).astype(BF)
            states.append(exchange.start(half))
        run(next(turn))
        projected = (matmul(x[b], unit(first, 0)) + narrow_out[b : b + 1]).astype(BF)
        query[b] = projected * jnp.asarray(score_scale, BF)
        stats[b] = jnp.zeros_like(stats[b])
        save("x", "query")
        for half in range(2):
            exchange.forward(half, states[half])
            exchange.finish(states[half])
            if half == 1:
                run(next(turn))
            attend(query.at[b], kvs[b], half, mask, mixed.at[b], stats.at[b], half * (HEADS // 2))
        run(next(turn))
        keep(kvs[b], kv_outs[b], save_sem.at[b, len(SAVED)])
        attended = matmul(mixed[b].astype(BF), unit(first, 3))
        hat, inverse = center_scale(carried[...] + attended + narrow_out[3 + 3 * b : 4 + 3 * b])
        hat_one[b] = hat
        lane = lax.broadcasted_iota(jnp.int32, stats.shape[1:], 1)
        stats[b] = jnp.where(lane == HEADS, inverse, stats[b])
        normed[...] = hat * narrow_out[8 + 2 * b : 9 + 2 * b] + narrow_out[12 + 2 * b : 13 + 2 * b]
        normed_bf[...] = normed[...].astype(BF)
        save("mixed", "hat_one")
        run(next(turn))
        for c in range(4):
            hidden = matmul(normed_bf[...], unit(second, c)) + wide_out[b, c : c + 1]
            cdf = 0.5 + 0.5 * lax.erf(hidden * (2.0**-0.5))
            pdf = jnp.exp(-0.5 * hidden * hidden) * ((2.0 * jnp.pi) ** -0.5)
            active[b, c] = (hidden * cdf).astype(BF)
            slope[b, c] = (cdf + hidden * pdf).astype(BF)
            run(next(turn))
        save("active", "slope")
        run(next(turn))
        update = normed[...] + narrow_out[4 + 3 * b : 5 + 3 * b]
        for c in range(4):
            update = update + matmul(active[b, c], third[c * n // 4 : (c + 1) * n // 4].reshape(D, D))
        hat, inverse = center_scale(update)
        hat_two[b] = hat
        stats[b] = jnp.where(lane == HEADS + 1, inverse, stats[b])
        save("stats", "hat_two")
        carried[...] = hat * narrow_out[9 + 2 * b : 10 + 2 * b] + narrow_out[13 + 2 * b : 14 + 2 * b]
        exchange.drain()
    result[...] = carried[...].astype(BF)
    for group in groups:
        group.drain()
    for copy in smalls:
        copy.wait_send()
    for copy in kept:
        copy.wait()


def forward_pass(n, ny, tokens, mask, qkv, ao, win, wout, *smalls):
    rows, width = tokens.shape[0], D // n
    nc = 2 * ny
    full_shapes = [(4, n, width, D), (4, n, width, D), (n, 4, width, D)] * 2
    kv_shape = (2, 2, nc, rows, D // 2)
    saved_shapes = {
        "x": ((2, rows, D), BF),
        "query": ((2, rows, D), BF),
        "mixed": ((2, rows, D), F32),
        "stats": ((2, rows, 128), F32),
        "hat_one": ((2, rows, D), F32),
        "active": ((2, 4, rows, D), BF),
        "slope": ((2, 4, rows, D), BF),
        "hat_two": ((2, rows, D), F32),
    }
    out = [jax.ShapeDtypeStruct(shape, BF) for shape in full_shapes]
    out += [jax.ShapeDtypeStruct(kv_shape, BF)] * 2
    out += [jax.ShapeDtypeStruct(*saved_shapes[name]) for name in SAVED]
    out += [
        jax.ShapeDtypeStruct((16, D), F32),
        jax.ShapeDtypeStruct((2, 4, D), F32),
        jax.ShapeDtypeStruct((rows, D), BF),
    ]
    anywhere = pl.BlockSpec(memory_space=pl.ANY)
    vmem = pl.BlockSpec(memory_space=pltpu.VMEM)
    scratch = [pltpu.VMEM(shape, BF) for shape in full_shapes]
    scratch += [pltpu.VMEM(kv_shape, BF)] * 2
    scratch += [pltpu.VMEM(*saved_shapes[name]) for name in SAVED]
    scratch += [
        pltpu.VMEM((rows, D), F32),
        pltpu.VMEM((rows, D), F32),
        pltpu.VMEM((rows, D), BF),
        pltpu.VMEM((n, 16, width), BF),
        pltpu.VMEM((n, 16, 4 * width), BF),
        pltpu.VMEM((16, width), F32),
        pltpu.VMEM((16, 4 * width), F32),
        pltpu.SemaphoreType.DMA((6, 5)),
        pltpu.SemaphoreType.DMA((6, Gather.count(n))),
        pltpu.SemaphoreType.DMA((6, Gather.count(n))),
        pltpu.SemaphoreType.DMA((2, n)),
        pltpu.SemaphoreType.DMA((2, n)),
        pltpu.SemaphoreType.DMA((2, 2, Exchange.count(ny))),
        pltpu.SemaphoreType.DMA((2, 2, Exchange.count(ny))),
        pltpu.SemaphoreType.DMA((2, len(SAVED) + 1)),
    ]
    return pl.pallas_call(
        functools.partial(forward_kernel, n, ny),
        out_shape=out,
        in_specs=[vmem, vmem] + [anywhere] * 4 + [vmem] * 5,
        out_specs=[anywhere] * 16 + [vmem] * 3,
        scratch_shapes=scratch,
        compiler_params=pltpu.CompilerParams(
            collective_id=0, has_side_effects=True, vmem_limit_bytes=60 * MIB
        ),
        name="forward_pass",
    )(tokens, mask, qkv, ao, win, wout, *smalls)


def normal_back(grad_output, gain, hat, inverse):
    grad_hat = grad_output * gain
    mean = jnp.mean(grad_hat, axis=-1, keepdims=True)
    slant = jnp.mean(grad_hat * hat, axis=-1, keepdims=True)
    return inverse * (grad_hat - mean - hat * slant)


def column_sum(rows):
    return jnp.sum(rows.astype(F32), axis=0, keepdims=True)


class KeyGrads:
    def __init__(self, place, grads, core_in, far_in, send, recv, credit):
        self.place, self.grads, self.core_in, self.far_in = place, grads, core_in, far_in
        self.send, self.recv, self.credit = send, recv, credit
        self.copies = []
        self.cored, self.far = {}, {}

    def peers(self):
        return [self.place.core()] + [self.place.row(o) for o in range(1, self.place.ny)]

    def release(self):
        for other in self.peers():
            pl.semaphore_signal(self.credit, inc=1, device_id=other, device_id_type=MESH)

    def acquire(self):
        pl.semaphore_wait(self.credit, len(self.peers()))

    @staticmethod
    def count(ny):
        return 2 * ny - 1

    def share(self, half, slot, src, dst, device):
        copy = remote(src, dst, self.send.at[half, slot], self.recv.at[half, slot], device)
        self.copies.append(copy)
        return copy

    def start(self, half):
        place, ny = self.place, self.place.ny
        self.cored[half] = []
        for i in range(ny):
            y = lax.rem(place.y + i, ny)
            part = self.grads.at[:, half, 2 * y + 1 - place.k]
            self.cored[half].append(self.share(half, i, part, self.core_in.at[:, half, y], place.core()))

    def middle(self, half):
        place, ny = self.place, self.place.ny
        for copy in self.cored[half]:
            copy.wait_recv()
        for y in range(ny):
            for kind in range(2):
                part = self.grads.at[kind, half, 2 * y + place.k]
                part[...] = (part[...].astype(F32) + self.core_in[kind, half, y].astype(F32)).astype(BF)
        self.far[half] = []
        for o in range(1, ny):
            y = lax.rem(place.y + o, ny)
            part = self.grads.at[:, half, 2 * y + place.k]
            self.far[half].append(
                self.share(half, ny + o - 1, part, self.far_in.at[:, half, o - 1], place.row(o))
            )

    def end(self, half, kind):
        for copy in self.far[half]:
            if kind == 0:
                copy.wait_recv()
        total = self.grads[kind, half, self.place.c].astype(F32)
        for o in range(1, self.place.ny):
            total = total + self.far_in[kind, half, o - 1].astype(F32)
        return total.astype(BF)

    def drain(self):
        for copy in self.copies:
            copy.wait_send()


def attend_back(query, kv, half, mask, stats, mixed, grad_mixed, grad_query, grads):
    rows = query.shape[0]
    lane = lax.broadcasted_iota(jnp.int32, (rows, 2 * HEAD), 1)
    blocks = 4 if kv.shape[2] <= 4 else 2

    def pair(p, _):
        columns = pl.ds(pl.multiple_of(p * 2 * HEAD, 2 * HEAD), 2 * HEAD)
        where = pl.ds(pl.multiple_of(half * (D // 2) + p * 2 * HEAD, 2 * HEAD), 2 * HEAD)
        query_pair, grad_pair = query[:, where], grad_mixed[:, where]
        products = (mixed[:, where] * grad_pair.astype(F32)).T
        grad_queries = [0.0, 0.0]
        for at in range(0, kv.shape[2], blocks):
            some = slice(at, at + blocks)
            keys = kv[0, half, some, :, columns].reshape(-1, 2 * HEAD)
            values = kv[1, half, some, :, columns].reshape(-1, 2 * HEAD)
            blocked = mask[at * rows : (at + blocks) * rows, :]
            grad_keys, grad_values = 0.0, 0.0
            for side in range(2):
                query_side, grad_side = query_pair * side_mask(side), grad_pair * side_mask(side)
                log_sum = stats[pl.ds(half * (HEADS // 2) + 2 * p + side, 1), :]
                inner = jnp.sum(products[side * HEAD : (side + 1) * HEAD], axis=0, keepdims=True)
                probs = jnp.exp(matmul_right_t(keys, query_side) + blocked - log_sum)
                grad_probs = matmul_right_t(values, grad_side)
                grad_scores = (probs * (grad_probs - inner)).astype(BF)
                grad_keys = grad_keys + matmul(grad_scores, query_side)
                grad_values = grad_values + matmul(probs.astype(BF), grad_side)
                grad_queries[side] = grad_queries[side] + matmul_left_t(grad_scores, keys)
            grads[0, half, some, :, columns] = grad_keys.astype(BF).reshape(-1, rows, 2 * HEAD)
            grads[1, half, some, :, columns] = grad_values.astype(BF).reshape(-1, rows, 2 * HEAD)
        grad_query[:, where] = (
            jnp.where(lane < HEAD, grad_queries[0], grad_queries[1]) * score_scale
        ).astype(BF)
        return 0

    lax.fori_loop(0, HEADS // 4, pair, 0)


ROWS = 12
PUMPS = [[1, 1, 1, 0, 0, 1, 0, 0], [1, 1, 1, 0, 0, 1, 0, 0]]
OUT_LATE, IN_LATE = [False, False], [True, False]


def backward_kernel(n, ny, *refs):
    upstream, mask, narrow = refs[:3]
    fulls, kvs, saved = refs[3:9], refs[9:11], refs[11:19]
    outs, out_small, out_tokens = refs[19:22], refs[22], refs[23]
    refs = refs[24:]
    window, held, kv = refs[0], refs[1:9], refs[9]
    grads, landings = refs[10:13], [refs[13 + 7 * i : 20 + 7 * i] for i in range(3)]
    refs = refs[34:]
    grad_kv, kv_core, kv_far = refs[:3]
    deeper, lower, update_rows, normed_rows, grad_query, grad_rows, stats_rows = refs[3:10]
    small_total, small_landing = refs[10:12]
    hidden = refs[12]
    carried = out_tokens
    load_sem, window_sem, local, send, recv, credit, kv_send, kv_recv, small_send, small_recv = refs[13:]
    place = Place(n, ny)
    roomy = ny == 2
    x, query, mixed, stats, hat_one, active, slope, hat_two = held
    if not roomy:
        hidden, update_rows, normed_rows = active, lower, lower
    ahead = window.shape[0]
    loads = {}

    def load(b, *names):
        for name in names:
            i = SAVED.index(name) if name != "kv" else len(SAVED)
            source, target = (kvs[b], kv) if name == "kv" else (saved[i].at[b], held[i])
            loads[(b, name)] = pltpu.make_async_copy(source, target, load_sem.at[i])
            loads[(b, name)].start()

    def ready(b, *names):
        for name in names:
            loads[(b, name)].wait()

    order = []
    for b in (1, 0):
        order += [(b, 2, c) for c in range(4)] + [(b, 1, c) for c in range(4)]
        order += [(b, 0, 3), (b, 0, 0), (b, 0, 1), (b, 0, 2)]
    fetched = []

    def fetch():
        i = len(fetched)
        if i < len(order):
            b, kind, c = order[i]
            copy = pltpu.make_async_copy(
                fulls[3 * b + kind].at[c], window.at[i % ahead], window_sem.at[i % ahead]
            )
            copy.start()
            fetched.append(copy)

    used = []

    def weight():
        i = len(used)
        if i > 0:
            fetch()
        fetched[i].wait()
        used.append(i)
        return window.at[i % ahead]

    load(1, "hat_two", "stats", "active", "slope", "hat_one", "mixed", "query", "kv", "x")
    for _ in range(ahead - 1):
        fetch()
    reduces = {}
    for b in (1, 0):
        for kind in range(3):
            g = 3 * b + kind
            reduces[(b, kind)] = Reduce(
                place,
                grads[kind],
                landings[kind],
                outs[kind].at[b],
                kind == 1,
                local.at[g],
                send.at[g],
                recv.at[g],
                credit.at[kind],
            )
    active_plans = []
    steps = {key: list(group.plan) for key, group in reduces.items()}

    def step(key):
        steps[key].pop(0)()
        if len(steps[key]) == 2 and key[0] == 1:
            reduces[key].release()

    def pump(count=1):
        for _ in range(count):
            for key in list(active_plans):
                step(key)
                if not steps[key]:
                    active_plans.remove(key)

    def complete(key):
        while steps[key]:
            pump()
        reduces[key].drain()

    def begin(b, kind):
        if b == 0:
            complete((1, kind))

    def sent(b, kind):
        active_plans.append((b, kind))

    place.greet()
    carried[...] = upstream[...].astype(F32)
    for b in (1, 0):
        third, second, first = [reduces[(b, kind)] for kind in (2, 1, 0)]

        def note(i, row, b=b):
            small_total[0, ROWS * b + i : ROWS * b + i + 1] = row

        turn = iter(PUMPS[b])
        gain_one, gain_two = narrow[8 + 2 * b : 9 + 2 * b], narrow[9 + 2 * b : 10 + 2 * b]
        ready(b, "hat_two", "stats", "active")
        stats_rows[...] = stats[...].T
        inverse_one, inverse_two = stats[:, HEADS : HEADS + 1], stats[:, HEADS + 1 : HEADS + 2]
        note(5, column_sum(carried[...] * hat_two[...]))
        note(7, column_sum(carried[...]))
        grad = normal_back(carried[...], gain_two, hat_two[...], inverse_two)
        deeper[...] = grad
        update_rows[...] = grad.astype(BF)
        note(3, column_sum(update_rows[...]))
        if b == 1:
            load(0, "hat_two")
        part = n // 4

        def out_grads(c):
            if c == 0:
                begin(b, 2)
            block = matmul_left_t(active[c], update_rows[...]).astype(BF)
            shards = pl.ds(c * part, part)
            grads[2][shards] = block.reshape(part, 4, D // n, D)
            if c == 0 and b == 0:
                third.acquire()
            third.core(shards, slice(None))
            if c == 3:
                sent(b, 2)

        def in_grads(c):
            if c == 0:
                begin(b, 1)
                normed_rows[...] = (hat_one[...] * gain_one + narrow[12 + 2 * b : 13 + 2 * b]).astype(BF)
            block = matmul_left_t(normed_rows[...], hidden[c]).astype(BF)
            grads[1][:, c] = block.reshape(n, D // n, D)
            if c == 0 and b == 0:
                second.acquire()
            second.core(slice(None), c)
            if c == 3:
                sent(b, 1)

        def attention_grads(i, left, right):
            if i == 3:
                begin(b, 0)
            block = matmul_left_t(left, right).astype(BF)
            grads[0][:, i] = block.reshape(n, D // n, D)
            if i == 3 and b == 0:
                first.acquire()
            first.core(slice(None), i)

        out_late, in_late = roomy and OUT_LATE[b], roomy and IN_LATE[b]
        if not out_late:
            for c in range(4):
                out_grads(c)
        ready(b, "slope", "hat_one")
        for c in range(4):
            flow = matmul_right_t(update_rows[...], weight()[...]) * slope[c].astype(F32)
            hidden[c] = flow.astype(BF)
            note(8 + c, column_sum(hidden[c]))
        if b == 1:
            load(0, "slope")
        pump(next(turn))
        if not in_late:
            for c in range(4):
                in_grads(c)
        pump(next(turn))
        for c in range(4):
            deeper[...] += matmul_right_t(hidden[c], weight()[...])
        note(4, column_sum(deeper[...] * hat_one[...]))
        note(6, column_sum(deeper[...]))
        carried[...] = normal_back(deeper[...], gain_one, hat_one[...], inverse_one)
        lower[...] = carried[...].astype(BF)
        note(2, column_sum(lower[...]))
        grad_rows[...] = matmul_right_t(lower[...], weight()[...]).astype(BF)
        pump(next(turn))
        ready(b, "mixed", "query", "kv")
        if not in_late:
            attention_grads(3, mixed[...].astype(BF), lower[...])
        keys = KeyGrads(place, grad_kv, kv_core, kv_far, kv_send.at[b], kv_recv.at[b], credit.at[3])
        if b == 0:
            keys.acquire()
        for half in range(2):
            attend_back(query, kv, half, mask, stats_rows, mixed, grad_rows, grad_query, grad_kv)
            keys.start(half)
            if half == 1:
                keys.middle(0)
            pump(next(turn))
        keys.middle(1)
        if out_late:
            for c in range(4):
                out_grads(c)
        pump(next(turn))
        if in_late:
            for c in range(4):
                in_grads(c)
            attention_grads(3, mixed[...].astype(BF), lower[...])
        if b == 1:
            load(0, "hat_one", "stats", "active", "mixed", "query", "kv")
        ready(b, "x")
        attention_grads(0, x[...], grad_query[...])
        note(0, column_sum(grad_query[...]))
        carried[...] += matmul_right_t(grad_query[...], weight()[...])
        pump(next(turn))
        for kind in range(2):
            for half in range(2):
                lower[:, half * (D // 2) : (half + 1) * (D // 2)] = keys.end(half, kind)
            attention_grads(1 + kind, x[...], lower[...])
            if kind == 1:
                note(1, column_sum(lower[...]))
            carried[...] += matmul_right_t(lower[...], weight()[...])
        sent(b, 0)
        pump(next(turn))
        keys.drain()
        if b == 1:
            keys.release()
            load(0, "x")
    small_sum = SmallReduce(place, small_total, small_landing, small_send, small_recv)
    small_steps = small_sum.steps()
    while active_plans or small_steps:
        if small_steps:
            small_steps.pop(0)()
        pump()
    out_small[...] = small_total[4]
    for key, group in reduces.items():
        group.finish()
        group.drain()
    for copy in small_sum.copies:
        copy.wait_send()


def backward_pass(n, ny, upstream, mask, narrow, fulls, kvs, saved):
    rows, width = upstream.shape[0], D // n
    nc = 2 * ny
    out = [jax.ShapeDtypeStruct((2,) + shape, BF) for shape in ((4, width, D), (width, 4 * D), (4, width, D))]
    out += [jax.ShapeDtypeStruct((2 * ROWS, D), F32), jax.ShapeDtypeStruct((rows, D), F32)]
    anywhere = pl.BlockSpec(memory_space=pl.ANY)
    vmem = pl.BlockSpec(memory_space=pltpu.VMEM)
    smalls = SmallReduce.count(n, ny)
    ahead = 4 if ny == 2 else 2
    scratch = [pltpu.VMEM((ahead, D, D), BF)]
    scratch += [pltpu.VMEM(item.shape[1:], item.dtype) for item in saved]
    scratch += [pltpu.VMEM(kvs[0].shape, BF)]
    scratch += [pltpu.VMEM((n, 4, width, D), BF)] * 3
    for _ in range(3):
        scratch += Reduce.landing_buffers(n, ny)
    scratch += [pltpu.VMEM((2, 2, nc, rows, D // 2), BF)]
    scratch += [pltpu.VMEM((2, 2, ny, rows, D // 2), BF), pltpu.VMEM((2, 2, ny - 1, rows, D // 2), BF)]
    scratch += [
        pltpu.VMEM((rows, D), F32),
        pltpu.VMEM((rows, D), BF),
        pltpu.VMEM((rows, D) if ny == 2 else (16, 128), BF),
        pltpu.VMEM((rows, D) if ny == 2 else (16, 128), BF),
        pltpu.VMEM((rows, D), BF),
        pltpu.VMEM((rows, D), BF),
        pltpu.VMEM((128, rows), F32),
        pltpu.VMEM((5, 2 * ROWS, D), F32),
        pltpu.VMEM((smalls, 2 * ROWS, D), F32),
        pltpu.VMEM((4, rows, D) if ny == 2 else (16, 128), BF),
        pltpu.SemaphoreType.DMA((len(SAVED) + 1,)),
        pltpu.SemaphoreType.DMA((ahead,)),
        pltpu.SemaphoreType.DMA((6,)),
        pltpu.SemaphoreType.DMA((6, Reduce.count(n, ny))),
        pltpu.SemaphoreType.DMA((6, Reduce.count(n, ny))),
        pltpu.SemaphoreType.REGULAR((4,)),
        pltpu.SemaphoreType.DMA((2, 2, KeyGrads.count(ny))),
        pltpu.SemaphoreType.DMA((2, 2, KeyGrads.count(ny))),
        pltpu.SemaphoreType.DMA((smalls,)),
        pltpu.SemaphoreType.DMA((smalls,)),
    ]
    return pl.pallas_call(
        functools.partial(backward_kernel, n, ny),
        out_shape=out,
        in_specs=[vmem] * 3 + [anywhere] * 16,
        out_specs=[anywhere] * 3 + [vmem] * 2,
        scratch_shapes=scratch,
        compiler_params=pltpu.CompilerParams(
            collective_id=1, has_side_effects=True, vmem_limit_bytes=63 * MIB
        ),
        name="backward_pass",
    )(upstream, mask, narrow, *fulls, *kvs, *saved)


def body(
    tokens,
    lengths,
    cotangent,
    w_qkv,
    w_attn_out,
    w_in,
    w_out,
    bias_q,
    bias_d,
    bias_ff,
    norm_gain,
    norm_shift,
    n,
    ny,
):
    row_count = tokens.shape[1]
    width = D // n
    z = lax.axis_index("fsdp")
    first_row = lax.axis_index("ctx") * row_count
    upstream = jnp.where((first_row + jnp.arange(row_count) < lengths[0])[:, None], cotangent[0], 0)
    mask = jnp.where(jnp.arange(2 * ny * row_count) < lengths[0], 0.0, masked_value).astype(F32)
    mask_row = jnp.broadcast_to(mask[None], (8, mask.shape[0]))
    made = forward_pass(
        n, ny, tokens[0], mask_row, w_qkv, w_attn_out, w_in, w_out.reshape(2, 4, width, D),
        bias_q, bias_d, bias_ff, norm_gain, norm_shift
    )
    fulls, kvs, saved = made[:6], made[6:8], made[8:16]
    narrow, _, result = made[16:]
    fulls = [full.reshape(4, D, D) for full in fulls]
    *sums, small_sum, grad_tokens = backward_pass(n, ny, upstream, mask[:, None], narrow, fulls, kvs, saved)
    small_sum = small_sum.reshape(2, ROWS, D)
    own = lax.dynamic_slice_in_dim(small_sum, z * width, width, 2)
    own_ff = lax.dynamic_slice_in_dim(small_sum[:, 8:].reshape(2, 4 * D), z * 4 * width, 4 * width, 1)
    return (
        result[None],
        grad_tokens[None],
        sums[0][:, :3].astype(F32),
        sums[0][:, 3].astype(F32),
        sums[1].astype(F32),
        sums[2].reshape(2, 4 * width, D).astype(F32),
        own[:, 0],
        own[:, 1:4],
        own_ff,
        own[:, 4:6],
        own[:, 6:8],
    )


def solution(mesh):
    placed = (
        P(("rep", "fsdp"), "ctx", None),
        P(("rep", "fsdp")),
        P(("rep", "fsdp"), "ctx", None),
        P(None, None, "fsdp", None),
        P(None, "fsdp", None),
        P(None, "fsdp", None),
        P(None, "fsdp", None),
        P(None, "fsdp"),
        P(None, None, "fsdp"),
        P(None, "fsdp"),
        P(None, None, "fsdp"),
        P(None, None, "fsdp"),
    )
    n, ny = mesh.shape["fsdp"], mesh.shape["ctx"] // 2
    return jax.shard_map(
        functools.partial(body, n=n, ny=ny),
        mesh=mesh,
        in_specs=placed,
        out_specs=(
            P(("rep", "fsdp"), "ctx", None),
            P(("rep", "fsdp"), "ctx", None),
            P(None, None, "fsdp", None),
            P(None, "fsdp", None),
            P(None, "fsdp", None),
            P(None, "fsdp", None),
            P(None, "fsdp"),
            P(None, None, "fsdp"),
            P(None, "fsdp"),
            P(None, None, "fsdp"),
            P(None, None, "fsdp"),
        ),
        check_vma=False,
    )
```

profile of v0, /device:TPU:0, one launch (start us, length us, event | category | flops | bytes accessed | tf_op | source)
XLA Modules:
  0.0 400.0 jit_solution(14537725720533798478)
XLA Ops:
  1.3 0.6 broadcast_in_dim.40.refs_1_
  1.9 1.3 copy.25.refs_7_
  3.2 0.0 copy-start.4
  3.2 147.6 %forward_pass.1 = (bf16[4,4,192,768]{3,2,1,0:T(8,128)(2,1)}, bf16[4,4,192,768]{3,2,1,0:T(8,128)(2,1)}, bf16[4,4,192,768]{3,2,1,0:T(8,128)(2,1)}, bf16[4,4,192,76...) custom-call(bf16[256,768]{1,0:T(8,128)(2,1)} %bitcast.36, ...), custom_call_target="tpu_custom_call" | custom-call | tf_op jit(solution)/shard_map/forward_pass/pallas_call | solution.py:737
  150.9 0.0 copy-done.4
  150.9 0.9 bitcast_select_fusion.refs_0_
  151.7 0.8 fusion.refs_1_
  152.6 231.5 %backward_pass.1 = (bf16[2,4,192,768]{3,2,1,0:T(8,128)(2,1)}, bf16[2,192,3072]{2,1,0:T(8,128)(2,1)}, bf16[2,4,192,768]{3,2,1,0:T(8,128)(2,1)}, f32[24,768]{1,0:T(8,128)}, f32[256,768]{1,0:T(8,128)}) custom-call(bf16[256,768]{1,0:T(8,128)(2,1)} %bitcast_select_fusion.refs_0_, f32[1024,1]{1,0:T(8,128)} %fusion.refs_1_, f32[16,768]{1,0:T(8,128)} %get-tuple-element.35.refs_2_, ...), custom_call_target="tpu_custom_call" | custom-call | tf_op jit(solution)/shard_map/backward_pass/pallas_call | solution.py:1146
  384.1 0.0 copy-start.1
  384.1 3.7 slice_convert_fusion
  387.8 2.2 bitcast_convert_fusion.1
  390.0 0.0 copy-done.1
  390.0 0.0 copy-start
  390.0 2.8 convert_element_type.23
  392.8 0.0 copy-done
  392.8 0.0 copy-start.5
  392.8 0.0 copy-start.3
  392.8 0.0 copy-start.2
  392.8 2.7 bitcast_convert_fusion
  395.5 0.0 copy-done.5
  395.5 0.1 constant_dynamic-slice_fusion.2
  395.6 0.6 copy.30
  396.2 0.1 constant_dynamic-slice_fusion.1
  396.2 0.6 copy.26
  396.9 0.6 constant_dynamic-slice_fusion.3
  397.5 0.7 constant_dynamic-slice_fusion.4
  398.1 0.0 copy-done.3
  398.1 0.7 copy.34
  398.9 0.0 copy-done.2
  398.9 0.9 copy.35
  (5 shorter events, 0.0 us)
Async XLA Ops:
  3.2 147.7 %copy-start.4 = (bf16[1,256,768]{2,1,0:T(8,128)(2,1)S(1)}, bf16[1,256,768]{2,1,0:T(8,128)(2,1)}, u32[]{:S(2)}) copy-start(bf16[1,256,768]{2,1,0:T(8,128)(2,1)} %param.14) | copy-start | bytes 1179652
  384.1 5.9 %copy-start.1 = (bf16[2,192,3072]{2,1,0:T(8,128)(2,1)S(1)}, bf16[2,192,3072]{2,1,0:T(8,128)(2,1)}, u32[]{:S(2)}) copy-start(bf16[2,192,3072]{2,1,0:T(8,128)(2,1)} %get-tuple-element.54) | copy-start | bytes 7077892
  390.0 2.8 copy-start
  392.8 2.7 copy-start.5
  392.8 5.4 %copy-start.3 = (bf16[256,768]{1,0:T(8,128)(2,1)S(1)}, bf16[256,768]{1,0:T(8,128)(2,1)}, u32[]{:S(2)}) copy-start(bf16[256,768]{1,0:T(8,128)(2,1)} %get-tuple-element.34) | copy-start | bytes 1179652
  392.8 6.1 %copy-start.2 = (f32[256,768]{1,0:T(8,128)S(1)}, f32[256,768]{1,0:T(8,128)}, u32[]{:S(2)}) copy-start(f32[256,768]{1,0:T(8,128)} %get-tuple-element.52) | copy-start | bytes 2359300
where the time goes:
time: 403 us; the launch traced here: 400 us
  Pallas kernels  379 us (94%)
  other arithmetic  13.1 us (3%)
  local copies, waits for them, and re-layouts  6.19 us (2%)
    pallas_call x1, Pallas kernels, backward_pass(): pl.pallas_call(functools.partial(backward_kernel, n, ny), out_shape=out,...  232 us
    pallas_call x1, Pallas kernels, forward_pass(): pl.pallas_call(functools.partial(forward_kernel, n, ny), out_shape=out, i...  148 us

commit v1 on v0

--- a/solution.py
+++ b/solution.py
@@ -860,7 +860,7 @@
 
 
 ROWS = 12
-PUMPS = [[1, 1, 1, 0, 0, 1, 0, 0], [1, 1, 1, 0, 0, 1, 0, 0]]
+PUMPS = [[1, 0, 0, 0, 0, 1, 0, 0], [1, 1, 1, 0, 0, 1, 0, 0]]
 OUT_LATE, IN_LATE = [False, False], [True, False]
 
 

time: 403 us -> 391 us (0.970)
  Pallas kernels: 379 us -> 367 us
    pallas_call x1, Pallas kernels: 232 us -> 219 us  [backward_pass(): pl.pallas_call(functools.partial(backward_kernel, n, ny), out_shape=out,...]
where the time goes in v1:
time: 391 us; the launch traced here: 387 us
  Pallas kernels  367 us (94%)
  other arithmetic  13.1 us (3%)
  local copies, waits for them, and re-layouts  6.19 us (2%)
    pallas_call x1, Pallas kernels, backward_pass(): pl.pallas_call(functools.partial(backward_kernel, n, ny), out_shape=out,...  219 us
    pallas_call x1, Pallas kernels, forward_pass(): pl.pallas_call(functools.partial(forward_kernel, n, ny), out_shape=out, i...  148 us

profile of v1, /device:TPU:0, one launch (start us, length us, event | category | flops | bytes accessed | tf_op | source)
XLA Modules:
  0.0 387.4 jit_solution(3480687739390217784)
XLA Ops:
  1.3 0.6 broadcast_in_dim.40.refs_1_
  1.9 1.3 copy.25.refs_7_
  3.2 0.0 copy-start.4
  3.2 147.6 %forward_pass.1 = (bf16[4,4,192,768]{3,2,1,0:T(8,128)(2,1)}, bf16[4,4,192,768]{3,2,1,0:T(8,128)(2,1)}, bf16[4,4,192,768]{3,2,1,0:T(8,128)(2,1)}, bf16[4,4,192,76...) custom-call(bf16[256,768]{1,0:T(8,128)(2,1)} %bitcast.36, ...), custom_call_target="tpu_custom_call" | custom-call | tf_op jit(solution)/shard_map/forward_pass/pallas_call | solution.py:737
  150.9 0.0 copy-done.4
  150.9 0.9 bitcast_select_fusion.refs_0_
  151.7 0.8 fusion.refs_1_
  152.6 218.9 %backward_pass.1 = (bf16[2,4,192,768]{3,2,1,0:T(8,128)(2,1)}, bf16[2,192,3072]{2,1,0:T(8,128)(2,1)}, bf16[2,4,192,768]{3,2,1,0:T(8,128)(2,1)}, f32[24,768]{1,0:T(8,128)}, f32[256,768]{1,0:T(8,128)}) custom-call(bf16[256,768]{1,0:T(8,128)(2,1)} %bitcast_select_fusion.refs_0_, f32[1024,1]{1,0:T(8,128)} %fusion.refs_1_, f32[16,768]{1,0:T(8,128)} %get-tuple-element.35.refs_2_, ...), custom_call_target="tpu_custom_call" | custom-call | tf_op jit(solution)/shard_map/backward_pass/pallas_call | solution.py:1146
  371.5 0.0 copy-start.1
  371.5 3.7 slice_convert_fusion
  375.2 2.2 bitcast_convert_fusion.1
  377.4 0.0 copy-done.1
  377.4 0.0 copy-start
  377.4 2.8 convert_element_type.23
  380.1 0.0 copy-done
  380.1 0.0 copy-start.5
  380.1 0.0 copy-start.3
  380.1 0.0 copy-start.2
  380.1 2.7 bitcast_convert_fusion
  382.8 0.0 copy-done.5
  382.9 0.1 constant_dynamic-slice_fusion.2
  382.9 0.6 copy.30
  383.5 0.1 constant_dynamic-slice_fusion.1
  383.6 0.6 copy.26
  384.2 0.6 constant_dynamic-slice_fusion.3
  384.8 0.7 constant_dynamic-slice_fusion.4
  385.5 0.0 copy-done.3
  385.5 0.7 copy.34
  386.3 0.0 copy-done.2
  386.3 0.9 copy.35
  (5 shorter events, 0.0 us)
Async XLA Ops:
  3.2 147.7 %copy-start.4 = (bf16[1,256,768]{2,1,0:T(8,128)(2,1)S(1)}, bf16[1,256,768]{2,1,0:T(8,128)(2,1)}, u32[]{:S(2)}) copy-start(bf16[1,256,768]{2,1,0:T(8,128)(2,1)} %param.14) | copy-start | bytes 1179652
  371.5 5.9 %copy-start.1 = (bf16[2,192,3072]{2,1,0:T(8,128)(2,1)S(1)}, bf16[2,192,3072]{2,1,0:T(8,128)(2,1)}, u32[]{:S(2)}) copy-start(bf16[2,192,3072]{2,1,0:T(8,128)(2,1)} %get-tuple-element.54) | copy-start | bytes 7077892
  377.4 2.8 copy-start
  380.1 2.7 copy-start.5
  380.1 5.4 %copy-start.3 = (bf16[256,768]{1,0:T(8,128)(2,1)S(1)}, bf16[256,768]{1,0:T(8,128)(2,1)}, u32[]{:S(2)}) copy-start(bf16[256,768]{1,0:T(8,128)(2,1)} %get-tuple-element.34) | copy-start | bytes 1179652
  380.1 6.1 %copy-start.2 = (f32[256,768]{1,0:T(8,128)S(1)}, f32[256,768]{1,0:T(8,128)}, u32[]{:S(2)}) copy-start(f32[256,768]{1,0:T(8,128)} %get-tuple-element.52) | copy-start | bytes 2359300
